TPU v7x, 32 devices: a whole 2x2x4 slice. The times are simulated.
32 devices in a mesh: freq: 4 (over x, core), rcv: 8 (over z, y).
Axes of the slice: x: 2, y: 2, z: 4, core: 2. Of those that a mesh axis runs over, the one named last changes fastest.
Arguments:
- spectra: bfloat16 [2, 128, 384, 1024], P(None, None, 'freq', 'rcv'), may hold values from -600 to 600
- valid: int32 [384, 1024], P(None, 'rcv'), may hold values from 0 to 1, as said below
- sources: int32 [32], P('rcv'), may hold values from 0 to 1023, as said below
- bounds: int32 [32, 1024, 2], P('freq', 'rcv'), may hold values from 0 to 128, as said below
Outputs:
- lag_corr: bfloat16 [32, 1024, 128], P('freq', 'rcv')
- peak_value: float32 [32, 1024], P('freq', 'rcv')
Inputs may be any that keep to these rules, and one draw needn't show every extreme that they name: `valid`: in each aligned group of 4 sub-windows at most one entry of a channel is 0. Source s is a channel from (s // 4) * 128 to (s // 4 + 1) * 128 - 1; the sources are distinct. bounds[s, c, 0] < bounds[s, c, 1] <= 128, and the window holds 16 to 64 lag samples.
All inputs are finite; a program needn't handle non-finite values.
Results may differ from a plain program's by a relative error of at most 0.007.
Values may be sent and summed in bfloat16 or wider, within the bound.
A program may use at most 128 MiB of HBM per device.

v0:
```python
import math

import jax
import jax.numpy as jnp
from jax import lax
from jax.sharding import PartitionSpec as P

L = 128


def make_tables(bin_first, bin_count, lag_count, period):
    bins_col = (bin_first + 1 + jnp.arange(bin_count, dtype=jnp.int32))[:, None]
    lag_row = jnp.arange(lag_count, dtype=jnp.int32)[None, :] - lag_count // 2
    phase_int = bins_col * lag_row % period
    angles = phase_int.astype(jnp.float32) * (2.0 * math.pi / period)
    return (jnp.cos(angles).astype(jnp.bfloat16), jnp.sin(angles).astype(jnp.bfloat16))


def local(spectra, valid, sources, bounds):
    freq_index = lax.axis_index("freq")
    rcv_index = lax.axis_index("rcv")
    freq_count = lax.axis_size("freq")
    window_rows = spectra.shape[2]
    channels = valid.shape[1]
    own_valid = lax.dynamic_slice_in_dim(valid, freq_index * window_rows, window_rows, 0).astype(
        jnp.float32
    )
    spectra_f = spectra.astype(jnp.float32)
    energy = jnp.mean(spectra_f[0] * spectra_f[0] + spectra_f[1] * spectra_f[1], axis=0)
    scaling = own_valid / jnp.sqrt(energy + 1e-06)
    whitened = (spectra_f * scaling).astype(jnp.bfloat16)
    regrouped = lax.all_to_all(whitened, "freq", split_axis=1, concat_axis=2, tiled=True)
    bins_dev = regrouped.shape[1]
    offsets = sources - rcv_index * channels
    picked = jnp.take(regrouped, offsets, axis=3)
    valid_half = valid.astype(jnp.bfloat16)
    picked_valid = jnp.take(valid_half, offsets, axis=1)[None, None]
    source_part = lax.all_gather(picked, "rcv", axis=3, tiled=True)
    source_valid = lax.all_gather(picked_valid, "rcv", axis=3, tiled=True)
    part_re = jnp.einsum(
        "fws,fwc->fsc", source_part[0], regrouped[0], preferred_element_type=jnp.float32
    )
    part_re = part_re + jnp.einsum(
        "fws,fwc->fsc", source_part[1], regrouped[1], preferred_element_type=jnp.float32
    )
    part_im = jnp.einsum(
        "fws,fwc->fsc", source_part[0], regrouped[1], preferred_element_type=jnp.float32
    )
    part_im = part_im - jnp.einsum(
        "fws,fwc->fsc", source_part[1], regrouped[0], preferred_element_type=jnp.float32
    )
    counts_part = jnp.einsum(
        "wn,wc->nc", source_valid[0, 0], valid_half, preferred_element_type=jnp.float32
    )
    stack_re = (part_re / counts_part).astype(jnp.bfloat16)
    stack_im = (part_im / counts_part).astype(jnp.bfloat16)
    period = 2 * bins_dev * freq_count
    whole_re, whole_im = (
        lax.all_to_all(stack_re, "freq", split_axis=1, concat_axis=0, tiled=True),
        lax.all_to_all(stack_im, "freq", split_axis=1, concat_axis=0, tiled=True),
    )
    full_cos, full_sin = make_tables(0, bins_dev * freq_count, L, period)
    corr_sum = jnp.einsum(
        "fsc,ft->sct", whole_re, full_cos, preferred_element_type=jnp.float32
    ) - jnp.einsum("fsc,ft->sct", whole_im, full_sin, preferred_element_type=jnp.float32)
    lag_corr = corr_sum.astype(jnp.bfloat16)
    lag_index = jnp.arange(L, dtype=jnp.int32)[None, None, :]
    inside = (lag_index >= bounds[:, :, 0:1]) & (lag_index < bounds[:, :, 1:2])
    peak_value = jnp.max(jnp.where(inside, lag_corr.astype(jnp.float32), -jnp.inf), axis=2)
    return (lag_corr, peak_value)


def solution(mesh):
    in_specs = (P(None, None, "freq", "rcv"), P(None, "rcv"), P("rcv"), P("freq", "rcv", None))
    out_specs = (P("freq", "rcv", None), P("freq", "rcv"))
    return jax.shard_map(local, mesh=mesh, in_specs=in_specs, out_specs=out_specs, check_vma=False)
```

profile of v0, /device:TPU:0, one launch (start us, length us, event | category | flops | bytes accessed | tf_op | source)
XLA Modules:
  0.0 196.3 jit_solution(12709465195682754128)
XLA Ops:
  7.2 4.6 %copy_convert_fusion = f32[2,128,96,128]{3,2,0,1:T(8,128)S(1)} fusion(bf16[2,128,96,128]{3,2,1,0:T(8,128)(2,1)} %param.4), kind=kLoop, calls=%fused_computation.7 | loop fusion | flops 3145728 | bytes 18874368 | tf_op jit(solution)/shard_map/convert_element_type | solution.py:28
  11.7 0.0 copy-start.2
  11.7 0.9 fusion.1
  12.7 0.0 copy-done.2
  12.7 7.2 %multiply_convert_fusion = bf16[2,128,96,128]{3,2,0,1:T(8,128)(2,1)} fusion(f32[96,128]{1,0:T(8,128)S(1)} %rsqrt_multiply_fusion, bf16[2,128,96,128]{3,2,1,0:T(8,128)(2,1)} %param.4), kind=kLoop, calls=%fused_computation.2 | loop fusion | flops 9437184 | bytes 12632064 | tf_op jit(solution)/shard_map/convert_element_type | solution.py:31
  20.0 0.0 copy-start.4
  20.0 5.4 %all-to-all-start = ((bf16[2,128,96,128]{3,2,0,1:T(8,128)(2,1)}), bf16[2,128,96,128]{3,2,0,1:T(8,128)(2,1)}, u32[]{:S(2)}, u32[]{:S(2)}) async-start(bf16[2,128,96,128]{3,2,0,1:T(8,128)(2,1)} %multiply_convert_fusion), calls=%async_computation | async-start | bytes 12582912 | tf_op jit(solution)/shard_map/all_to_all | solution.py:32
  25.4 0.0 all-gather.2.cloned.1.call-start
  25.4 0.0 copy-done.4
  25.4 71.2 %all-to-all-done = bf16[2,128,96,128]{3,2,0,1:T(8,128)(2,1)} async-done(((bf16[2,128,96,128]{3,2,0,1:T(8,128)(2,1)}), bf16[2,128,96,128]{3,2,0,1:T(8,128)(2,1)}, u32[]{:S(2)}, u32[]{:S(2)}) %all-to-all-start) | async-done | bytes 6291488 | tf_op jit(solution)/shard_map/all_to_all | solution.py:32
  96.7 7.4 %copy.50 = bf16[2,32,4,96,128]{4,3,2,1,0:T(8,128)(2,1)} copy(bf16[2,32,4,96,128]{4,3,0,1,2:T(8,128)(2,1)} %bitcast.2) | data formatting | bytes 12582912 | tf_op jit(solution)/shard_map/all_to_all | solution.py:32
  104.1 9.1 %copy.51 = bf16[2,32,384,128]{2,1,0,3:T(8,128)(2,1)} copy(bf16[2,32,384,128]{3,2,1,0:T(8,128)(2,1)} %bitcast.50) | data formatting | bytes 12582912 | tf_op jit(solution)/shard_map/all_to_all | solution.py:32
  113.2 3.4 %gather_fusion = bf16[4,2,32,384]{3,2,1,0:T(8,128)(2,1)S(1)} fusion(bf16[2,32,384,128]{2,1,0,3:T(8,128)(2,1)} %copy.51, s32[1024]{0:T(1024)S(1)} %pad_clamp_fusion), kind=kCustom, calls=%fused_computation | custom fusion | bytes 393232 | tf_op jit(solution)/shard_map/jit(_take)/gather | solution.py:35
  116.6 0.8 select_bitcast_fusion
  117.3 0.0 all-gather.2.cloned.1.call-update
  117.3 0.1 copy.56
  117.5 0.6 gather_fusion.1
  118.1 0.1 bitcast_select_fusion
  118.2 31.9 %all_gather.7 = bf16[1,1,384,32]{2,1,0,3:T(2,128)(2,1)S(1)} all-gather(bf16[1,1,384,4]{2,1,0,3:T(2,128)(2,1)S(1)} %copy.57), channel_id=1, replica_groups=mesh['freq'=4,'rcv'=8] {'rcv'}, dimensions={3}, use_global_device_ids=true | all-gather | bytes 27648 | tf_op jit(solution)/shard_map/all_gather | solution.py:39
  150.0 0.1 fusion.20
  150.2 4.0 %copy.49 = bf16[2,128,96,128]{3,2,1,0:T(8,128)(2,1)S(1)} copy(bf16[2,128,96,128]{3,2,0,1:T(8,128)(2,1)} %all-to-all-done) | data formatting | bytes 12582912 | tf_op jit(solution)/shard_map/all_to_all | solution.py:32
  154.1 1.4 fusion.31
  155.5 0.4 copy.53
  155.9 2.1 %copy.55 = bf16[1,32,4,96,128]{4,3,2,1,0:T(8,128)(2,1)} copy(bf16[1,32,4,96,128]{4,3,1,2,0:T(8,128)(2,1)S(1)} %get-tuple-element.16) | data formatting | bytes 6291456 | tf_op jit(solution)/shard_map/slice | solution.py:44
  158.0 4.6 %all-gather.2.cloned.1.call-done = bf16[2,32,384,32]{2,1,0,3:T(8,128)(2,1)} async-done(((bf16[2,32,384,4]{2,1,0,3:T(8,128)(2,1)}), bf16[2,32,384,32]{2,1,0,3:T(8,128)(2,1)}) %all-gather.2.cloned.1.call-update) | async-done | bytes 1572880 | tf_op jit(solution)/shard_map/all_gather | solution.py:38
  162.6 0.0 copy-start
  162.6 1.7 fusion.32
  164.3 0.0 copy-start.1
  164.3 0.8 fusion.8
  165.1 0.0 copy-done
  165.1 1.5 fusion.7
  166.6 0.0 copy-start.3
  166.6 0.7 fusion.6
  167.3 0.0 copy-done.1
  167.3 0.8 copy.58
  168.1 3.4 %all-to-all-start.1 = ((bf16[32,32,128]{2,0,1:T(8,128)(2,1)}), bf16[32,32,128]{2,0,1:T(8,128)(2,1)S(1)}, u32[]{:S(2)}, u32[]{:S(2)}) async-start(bf16[32,32,128]{2,0,1:T(8,128)(2,1)} %copy.58), calls=%async_computation.1 | async-start | bytes 524288 | tf_op jit(solution)/shard_map/all_to_all | solution.py:59
  171.5 2.0 %fusion.5 = bf16[32,32,128]{2,1,0:T(8,128)(2,1)S(1)} fusion(f32[32,32,128]{2,1,0:T(8,128)} %fusion.7, bf16[32,384,128]{2,1,0:T(8,128)(2,1)S(1)} %bitcast.52, bf16[1,32,384,32]{2,1,0,3:T(8,128)(2,1)} %copy-done.1, f32[32,128]{1,0:T(8,128)S(1)} %fusion.20), kind=kOutput, calls=%fused_computation.14 | convolution fusion | flops 101056512 | bytes 4734976 | tf_op jit(solution)/shard_map/fws,fwc->fsc/dot_general | solution.py:49
  173.5 0.8 copy.60
  174.4 3.2 %all-to-all-done.1 = bf16[32,32,128]{2,0,1:T(8,128)(2,1)S(1)} async-done(((bf16[32,32,128]{2,0,1:T(8,128)(2,1)}), bf16[32,32,128]{2,0,1:T(8,128)(2,1)S(1)}, u32[]{:S(2)}, u32[]{:S(2)}) %all-to-all-start.1) | async-done | bytes 262176 | tf_op jit(solution)/shard_map/all_to_all | solution.py:59
  177.6 3.4 %all-to-all-start.2 = ((bf16[32,32,128]{2,0,1:T(8,128)(2,1)}), bf16[32,32,128]{2,0,1:T(8,128)(2,1)S(1)}, u32[]{:S(2)}, u32[]{:S(2)}) async-start(bf16[32,32,128]{2,0,1:T(8,128)(2,1)} %copy.60), calls=%async_computation.2 | async-start | bytes 524288 | tf_op jit(solution)/shard_map/all_to_all | solution.py:60
  181.0 0.0 copy-done.3
  181.0 5.9 %all-to-all-done.2 = bf16[32,32,128]{2,0,1:T(8,128)(2,1)S(1)} async-done(((bf16[32,32,128]{2,0,1:T(8,128)(2,1)}), bf16[32,32,128]{2,0,1:T(8,128)(2,1)S(1)}, u32[]{:S(2)}, u32[]{:S(2)}) %all-to-all-start.2) | async-done | bytes 262176 | tf_op jit(solution)/shard_map/all_to_all | solution.py:60
  187.0 0.5 fusion.14
  187.5 1.1 select_reduce_fusion
  188.6 0.8 copy.62
  (9 shorter events, 0.1 us)
Async XLA Ops:
  11.7 1.0 copy-start.2
  20.0 5.5 %copy-start.4 = (s32[4]{0:T(128)S(1)}, s32[4]{0:T(128)}, u32[]{:S(2)}) copy-start(s32[4]{0:T(128)} %param.6) | copy-start | bytes 52
  20.0 76.7 %all-to-all-start = ((bf16[2,128,96,128]{3,2,0,1:T(8,128)(2,1)}), bf16[2,128,96,128]{3,2,0,1:T(8,128)(2,1)}, u32[]{:S(2)}, u32[]{:S(2)}) async-start(bf16[2,128,96,128]{3,2,0,1:T(8,128)(2,1)} %multiply_convert_fusion), calls=%async_computation | async-start | bytes 12582912 | tf_op jit(solution)/shard_map/all_to_all | solution.py:32
  25.4 137.3 %all-gather.2.cloned.1.call-start = ((), (), s32[]{:S(2)}) async-start(), calls=%async_computation.3 | async-start | bytes 1769472 | tf_op jit(solution)/shard_map/all_gather | solution.py:38
  162.6 2.5 %copy-start = (bf16[1,32,4,96,128]{4,3,2,1,0:T(8,128)(2,1)S(1)}, bf16[1,32,4,96,128]{4,3,2,1,0:T(8,128)(2,1)}, u32[]{:S(2)}) copy-start(bf16[1,32,4,96,128]{4,3,2,1,0:T(8,128)(2,1)} %copy.55) | copy-start | bytes 9437188
  164.3 3.0 %copy-start.1 = (bf16[1,32,384,32]{2,1,0,3:T(8,128)(2,1)}, bf16[1,32,384,32]{2,1,0,3:T(8,128)(2,1)S(1)}, u32[]{:S(2)}) copy-start(bf16[1,32,384,32]{2,1,0,3:T(8,128)(2,1)S(1)} %get-tuple-element.18) | copy-start | bytes 2359300
  166.6 14.4 %copy-start.3 = (s32[8,128,2]{1,2,0:T(2,128)S(1)}, s32[8,128,2]{1,2,0:T(2,128)}, u32[]{:S(2)}) copy-start(s32[8,128,2]{1,2,0:T(2,128)} %param.7) | copy-start | bytes 24580
  168.1 9.4 %all-to-all-start.1 = ((bf16[32,32,128]{2,0,1:T(8,128)(2,1)}), bf16[32,32,128]{2,0,1:T(8,128)(2,1)S(1)}, u32[]{:S(2)}, u32[]{:S(2)}) async-start(bf16[32,32,128]{2,0,1:T(8,128)(2,1)} %copy.58), calls=%async_computation.1 | async-start | bytes 524288 | tf_op jit(solution)/shard_map/all_to_all | solution.py:59
  177.6 9.4 %all-to-all-start.2 = ((bf16[32,32,128]{2,0,1:T(8,128)(2,1)}), bf16[32,32,128]{2,0,1:T(8,128)(2,1)S(1)}, u32[]{:S(2)}, u32[]{:S(2)}) async-start(bf16[32,32,128]{2,0,1:T(8,128)(2,1)} %copy.60), calls=%async_computation.2 | async-start | bytes 524288 | tf_op jit(solution)/shard_map/all_to_all | solution.py:60
Sparse Core Ops, SparseCore 0:
  117.5 45.0 all-gather.1
where the time goes:
time: 197 us; the launch traced here: 196 us
  waiting for transfers between devices  85 us (43%)
  local copies, waits for them, and re-layouts  32.6 us (17%)
  blocking collectives  31.9 us (16%)
  between operations  14.3 us (7%)
  other arithmetic  13.6 us (7%)
  starting transfers between devices  12.2 us (6%)
  matrix products  6.72 us (3%)
    all_to_all x1, waiting for transfers between devices, local(): lax.all_to_all(whitened, 'freq', split_axis=1, concat_axis=2, tiled=True)  71.2 us
    all_gather x1, blocking collectives, local(): source_valid = lax.all_gather(picked_valid, 'rcv', axis=3, tiled=True)  31.9 us
    all_to_all x3, local copies, waits for them, and re-layouts, local(): lax.all_to_all(whitened, 'freq', split_axis=1, concat_axis=2, tiled=True)  20.5 us
    convert_element_type x1, other arithmetic, local(): whitened = (spectra_f * scaling).astype(jnp.bfloat16)  7.22 us
    all_to_all x1, waiting for transfers between devices, local(): lax.all_to_all(stack_im, 'freq', split_axis=1, concat_axis=0, tiled=True)  5.95 us
    all_to_all x1, starting transfers between devices, local(): lax.all_to_all(whitened, 'freq', split_axis=1, concat_axis=2, tiled=True)  5.38 us
    all_gather x1, waiting for transfers between devices, local(): source_part = lax.all_gather(picked, 'rcv', axis=3, tiled=True)  4.61 us
    convert_element_type x1, other arithmetic, local(): spectra_f = spectra.astype(jnp.float32)  4.56 us
  transfers between devices with their start and end apart: 4, of which 4 were waited for; matrix products, arithmetic and copies ran while one was open for 6% of the time, Pallas kernels for 0%

commit v1 on v0

v1 whole, which is shorter than its diff:
```python
import math

import jax
import jax.numpy as jnp
from jax import lax
from jax.sharding import PartitionSpec as P

L = 128


def make_tables(bin_count, lag_count, period):
    bins_col = (1 + jnp.arange(bin_count, dtype=jnp.int32))[:, None]
    lag_row = jnp.arange(lag_count, dtype=jnp.int32)[None, :] - lag_count // 2
    phase_int = bins_col * lag_row % period
    angles = phase_int.astype(jnp.float32) * (2.0 * math.pi / period)
    return (jnp.cos(angles).astype(jnp.bfloat16), jnp.sin(angles).astype(jnp.bfloat16))


def local(spectra, valid, sources, bounds):
    freq_index = lax.axis_index("freq")
    rcv_index = lax.axis_index("rcv")
    window_rows = spectra.shape[2]
    channels = valid.shape[1]
    bins = spectra.shape[1]
    own_valid = lax.dynamic_slice_in_dim(valid, freq_index * window_rows, window_rows, 0).astype(
        jnp.float32
    )
    spectra_f = spectra.astype(jnp.float32)
    energy = jnp.mean(spectra_f[0] * spectra_f[0] + spectra_f[1] * spectra_f[1], axis=0)
    scaling = own_valid / jnp.sqrt(energy + 1e-06)
    whitened = (spectra_f * scaling).astype(jnp.bfloat16)
    offsets = sources - rcv_index * channels
    onehot = (offsets[:, None] == jnp.arange(channels, dtype=jnp.int32)[None, :]).astype(jnp.bfloat16)
    valid_half = valid.astype(jnp.bfloat16)
    picked = jnp.einsum("pfwc,sc->fspw", whitened, onehot)
    picked_valid = jnp.einsum("wc,sc->sw", valid_half, onehot)
    source_part = lax.all_gather(picked, "rcv", axis=1, tiled=True)
    source_valid = lax.all_gather(picked_valid, "rcv", axis=0, tiled=True)
    swapped = jnp.stack([whitened[1], -whitened[0]], axis=0)
    part_re = jnp.einsum("fspw,pfwc->fsc", source_part, whitened, preferred_element_type=jnp.float32)
    part_im = jnp.einsum("fspw,pfwc->fsc", source_part, swapped, preferred_element_type=jnp.float32)
    counts = jnp.einsum("sw,wc->sc", source_valid, valid_half, preferred_element_type=jnp.float32)
    stack_re = (part_re / counts).astype(jnp.bfloat16)
    stack_im = (part_im / counts).astype(jnp.bfloat16)
    full_cos, full_sin = make_tables(bins, L, 2 * bins)
    partial = jnp.einsum(
        "fsc,ft->sct", stack_re, full_cos, preferred_element_type=jnp.float32
    ) - jnp.einsum("fsc,ft->sct", stack_im, full_sin, preferred_element_type=jnp.float32)
    lag_sum = lax.psum_scatter(partial, "freq", scatter_dimension=0, tiled=True)
    lag_corr = lag_sum.astype(jnp.bfloat16)
    lag_index = jnp.arange(L, dtype=jnp.int32)[None, None, :]
    inside = (lag_index >= bounds[:, :, 0:1]) & (lag_index < bounds[:, :, 1:2])
    peak_value = jnp.max(jnp.where(inside, lag_corr.astype(jnp.float32), -jnp.inf), axis=2)
    return (lag_corr, peak_value)


def solution(mesh):
    in_specs = (P(None, None, "freq", "rcv"), P(None, "rcv"), P("rcv"), P("freq", "rcv", None))
    out_specs = (P("freq", "rcv", None), P("freq", "rcv"))
    return jax.shard_map(local, mesh=mesh, in_specs=in_specs, out_specs=out_specs, check_vma=False)
```

time: 197 us -> 136 us (0.69)
  waiting for transfers between devices: 85 us -> 38.5 us
  local copies, waits for them, and re-layouts: 32.6 us -> 9.22 us
  matrix products: 6.72 us -> 20.2 us
  starting transfers between devices: 12.2 us -> 0.08 us
  other arithmetic: 13.6 us -> 21 us
    all_to_all x3 -> x0, waiting for transfers between devices: 80.4 us -> none  [the longest x1 71.2 us: local(): lax.all_to_all(whitened, 'freq', split_axis=1, concat_axis=2, tiled=True)]
    reduce_scatter x0 -> x1, waiting for transfers between devices: none -> 30.3 us  [local(): lag_sum = lax.psum_scatter(partial, 'freq', scatter_dimension=0, tiled=True)]
    all_to_all x5 -> x0, local copies, waits for them, and re-layouts: 20.5 us -> none  [the longest x3 20.5 us: local(): lax.all_to_all(whitened, 'freq', split_axis=1, concat_axis=2, tiled=True)]
    dot_general x7, matrix products: 6.72 us -> 20.2 us  [the longest x1 6.66 us: local(): jnp.einsum('fspw,pfwc->fsc', source_part, whitened, preferred_element_typ...]
    all_to_all x3 -> x0, starting transfers between devices: 12.2 us -> none  [the longest x1 5.38 us: local(): lax.all_to_all(whitened, 'freq', split_axis=1, concat_axis=2, tiled=True)]
    slice x0 -> x1, other arithmetic: none -> 6.13 us  [local(): swapped = jnp.stack([whitened[1], -whitened[0]], axis=0)]
    slice x4 -> x0, local copies, waits for them, and re-layouts: 5.54 us -> none  [the longest x2 3.45 us: local(): regrouped[1]]
    dot_general x0 -> x2, local copies, waits for them, and re-layouts: none -> 5.04 us  [the longest x1 3.17 us: local(): jnp.einsum('fspw,pfwc->fsc', source_part, swapped, preferred_element_type...]
  transfers between devices with their start and end apart: 4 -> 2, of which waited for: 4 -> 2; matrix products, arithmetic and copies ran while one was open for 6% -> 5% of each run, Pallas kernels for 0% -> 0%
where the time goes in v1:
time: 136 us
  waiting for transfers between devices  38.5 us (28%)
  blocking collectives  32.4 us (24%)
  other arithmetic  21 us (15%)
  matrix products  20.2 us (15%)
  between operations  14.2 us (10%)
  local copies, waits for them, and re-layouts  9.22 us (7%)
    all_gather x1, blocking collectives, local(): source_valid = lax.all_gather(picked_valid, 'rcv', axis=0, tiled=True)  32.4 us
    reduce_scatter x1, waiting for transfers between devices, local(): lag_sum = lax.psum_scatter(partial, 'freq', scatter_dimension=0, tiled=True)  30.3 us
    all_gather x1, waiting for transfers between devices, local(): source_part = lax.all_gather(picked, 'rcv', axis=1, tiled=True)  8.16 us
    convert_element_type x1, other arithmetic, local(): whitened = (spectra_f * scaling).astype(jnp.bfloat16)  6.68 us
    dot_general x1, matrix products, local(): jnp.einsum('fspw,pfwc->fsc', source_part, whitened, preferred_element_typ...  6.66 us
    slice x1, other arithmetic, local(): swapped = jnp.stack([whitened[1], -whitened[0]], axis=0)  6.13 us
    dot_general x1, matrix products, local(): picked = jnp.einsum('pfwc,sc->fspw', whitened, onehot)  4.61 us
    convert_element_type x1, other arithmetic, local(): spectra_f = spectra.astype(jnp.float32)  4.56 us
  transfers between devices with their start and end apart: 2, of which 2 were waited for; matrix products, arithmetic and copies ran while one was open for 5% of the time, Pallas kernels for 0%

profile of v1, /device:TPU:0, one launch (start us, length us, event | category | flops | bytes accessed | tf_op | source)
XLA Modules:
  0.0 135.6 jit_solution(761228631241474031)
XLA Ops:
  7.2 0.0 all-gather.3.cloned.1.call-start
  7.2 4.6 %convert_element_type.36 = f32[2,128,96,128]{3,2,1,0:T(8,128)S(1)} convert(bf16[2,128,96,128]{3,2,1,0:T(8,128)(2,1)} %param.4) | non-fusion elementwise | flops 3145728 | bytes 18874368 | tf_op jit(solution)/shard_map/convert_element_type | solution.py:28
  11.8 0.0 copy-start.4
  11.8 0.9 fusion.1
  12.7 0.0 copy-done.4
  12.8 0.0 copy-start.6
  12.8 6.7 %multiply_convert_fusion = bf16[2,128,96,128]{3,2,1,0:T(8,128)(2,1)} fusion(f32[96,128]{1,0:T(8,128)S(1)} %rsqrt_multiply_fusion, bf16[2,128,96,128]{3,2,1,0:T(8,128)(2,1)} %param.4), kind=kLoop, calls=%fused_computation | loop fusion | flops 9437184 | bytes 12632064 | tf_op jit(solution)/shard_map/convert_element_type | solution.py:31
  19.5 0.0 copy-done.6
  19.5 4.6 %fusion.10 = bf16[128,4,2,96]{0,1,3,2:T(4,128)(2,1)S(1)} fusion(bf16[2,128,96,128]{3,2,1,0:T(8,128)(2,1)} %multiply_convert_fusion, s32[4]{0:T(128)S(1)} %broadcast_subtract_fusion), kind=kOutput, calls=%fused_computation.18 | convolution fusion | flops 25166336 | bytes 6488080 | tf_op jit(solution)/shard_map/pfwc,sc->fspw/dot_general | solution.py:35
  24.1 0.7 copy.8
  24.8 0.0 all-gather.3.cloned.1.call-update
  24.8 0.0 reduce-scatter.2.cloned.1.call-start
  24.9 0.2 convolution_bitcast_fusion
  25.0 32.4 %all-gather = bf16[8,4,384]{2,1,0:T(4,128)(2,1)S(1)} all-gather(bf16[1,4,384]{2,1,0:T(4,128)(2,1)S(1)} %convolution_bitcast_fusion), channel_id=1, replica_groups=mesh['freq'=4,'rcv'=8] {'rcv'}, dimensions={0}, use_global_device_ids=true | all-gather | bytes 27648 | tf_op jit(solution)/shard_map/all_gather | solution.py:38
  57.5 0.1 fusion.20
  57.6 6.1 %fusion.41 = (bf16[1,128,96,128]{3,2,1,0:T(8,128)(2,1)}, bf16[1,128,96,128]{3,2,1,0:T(8,128)(2,1)}) fusion(bf16[2,128,96,128]{3,2,1,0:T(8,128)(2,1)} %multiply_convert_fusion), kind=kLoop, calls=%fused_computation.56 | loop fusion | flops 1572864 | bytes 12582912 | tf_op jit(solution)/shard_map/slice | solution.py:39
  63.7 8.2 %all-gather.3.cloned.1.call-done = bf16[128,32,2,96]{0,3,2,1:T(8,128)(2,1)} async-done(((bf16[128,4,2,96]{0,3,2,1:T(8,128)(2,1)}), bf16[128,32,2,96]{0,3,2,1:T(8,128)(2,1)}) %all-gather.3.cloned.1.call-update) | async-done | bytes 1572880 | tf_op jit(solution)/shard_map/all_gather | solution.py:37
  71.9 3.4 %copy.10 = bf16[128,32,2,96]{3,1,2,0:T(8,128)(2,1)S(1)} copy(bf16[128,32,2,96]{0,3,2,1:T(8,128)(2,1)} %all-gather.3.cloned.1.call-done) | data formatting | bytes 3145728 | tf_op jit(solution)/shard_map/all_gather | solution.py:37
  75.3 0.0 copy-start.1
  75.3 0.0 copy-start.2
  75.3 6.7 %fusion.4 = f32[128,32,128,1]{2,1,3,0:T(8,128)} fusion(bf16[128,32,2,96]{3,1,2,0:T(8,128)(2,1)S(1)} %copy.10, bf16[2,128,96,128]{3,2,1,0:T(8,128)(2,1)} %multiply_convert_fusion), kind=kOutput, calls=%fused_computation.8 | convolution fusion | flops 201326592 | bytes 9961472 | tf_op jit(solution)/shard_map/fspw,pfwc->fsc/dot_general | solution.py:40
  82.0 0.0 copy-done.1
  82.0 0.0 copy-done.2
  82.0 3.6 %fusion.2 = f32[128,32,128,1]{2,1,3,0:T(8,128)} fusion(bf16[128,32,2,96]{3,1,2,0:T(8,128)(2,1)S(1)} %copy.10, bf16[1,128,96,128]{3,2,1,0:T(8,128)(2,1)S(1)} %copy-done.2, bf16[1,128,96,128]{3,2,1,0:T(8,128)(2,1)S(1)} %copy-done.1), kind=kOutput, calls=%fused_computation.6 | convolution fusion | flops 204472320 | bytes 9961472 | tf_op jit(solution)/shard_map/fspw,pfwc->fsc/dot_general | solution.py:41
  85.6 0.0 copy-start
  85.6 3.2 %copy.14 = f32[128,32,128,1]{0,2,1,3:T(8,128)} copy(f32[128,32,128,1]{2,1,3,0:T(8,128)} %fusion.2) | data formatting | bytes 4194304 | tf_op jit(solution)/shard_map/fspw,pfwc->fsc/dot_general | solution.py:41
  88.7 0.0 copy-done
  88.7 1.9 %copy.12 = f32[128,32,128,1]{0,2,1,3:T(8,128)} copy(f32[128,32,128,1]{2,1,3,0:T(8,128)S(1)} %copy-done) | data formatting | bytes 4194304 | tf_op jit(solution)/shard_map/fspw,pfwc->fsc/dot_general | solution.py:40
  90.6 0.0 copy-start.3
  90.6 2.7 %fusion.14 = f32[32,128,128]{2,1,0:T(8,128)S(1)} fusion(f32[128,32,128,1]{0,2,1,3:T(8,128)} %copy.12, f32[32,128]{1,0:T(8,128)S(1)} %fusion.20, s32[128]{0:T(128)S(1)} %get-tuple-element.8, s32[128]{0:T(128)S(1)} %get-tuple-element.9), kind=kOutput, calls=%fused_computation.20 | convolution fusion | flops 135512064 | bytes 4211712 | tf_op jit(solution)/shard_map/fsc,ft->sct/dot_general | solution.py:46
  93.3 0.0 copy-done.3
  93.3 0.0 copy-start.5
  93.4 2.3 %convolution_subtract_fusion = f32[32,128,128]{2,1,0:T(8,128)} fusion(f32[32,128,128]{2,1,0:T(8,128)S(1)} %fusion.14, f32[128,32,128,1]{0,2,1,3:T(8,128)S(1)} %copy-done.3, f32[32,128]{1,0:T(8,128)S(1)} %fusion.20, s32[128]{0:T(128)S(1)} %get-tuple-element.8, s32[128]{0:T(128)S(1)} %get-tuple-element.9), kind=kOutput, calls=%fused_computation.17 | convolution fusion | flops 136036352 | bytes 6308864 | tf_op jit(solution)/shard_map/fsc,ft->sct/dot_general | solution.py:48
  95.7 0.0 reduce-scatter.2.cloned.1.call-update
  95.7 0.0 copy-done.5
  95.7 30.3 %reduce-scatter.2.cloned.1.call-done = f32[8,128,128]{2,1,0:T(8,128)} async-done(((f32[32,128,128]{2,1,0:T(8,128)}), f32[8,128,128]{2,1,0:T(8,128)}) %reduce-scatter.2.cloned.1.call-update) | async-done | bytes 524304 | tf_op jit(solution)/shard_map/reduce_scatter | solution.py:49
  126.1 2.7 %select_reduce_fusion = (f32[8,128]{1,0:T(8,128)}, bf16[8,128,128]{2,1,0:T(8,128)(2,1)}) fusion(s32[8,128]{1,0:T(8,128)S(1)} %bitcast.31, s32[8,128]{1,0:T(8,128)S(1)} %bitcast.30, f32[8,128,128]{2,1,0:T(8,128)} %reduce-scatter.2.cloned.1.call-done), kind=kLoop, calls=%fused_computation.21 | loop fusion | flops 916480 | bytes 798720 | tf_op jit(solution)/shard_map/reduce_max | solution.py:53
  (5 shorter events, 0.0 us)
Async XLA Ops:
  7.2 64.7 %all-gather.3.cloned.1.call-start = ((), (), s32[]{:S(2)}) async-start(), calls=%async_computation.1 | async-start | bytes 1769472 | tf_op jit(solution)/shard_map/all_gather | solution.py:37
  11.8 1.0 copy-start.4
  12.8 6.7 %copy-start.6 = (s32[4]{0:T(128)S(1)}, s32[4]{0:T(128)}, u32[]{:S(2)}) copy-start(s32[4]{0:T(128)} %param.6) | copy-start | bytes 52
  24.8 101.3 %reduce-scatter.2.cloned.1.call-start = ((), (), s32[]{:S(2)}) async-start(), calls=%async_computation.2 | async-start | bytes 2621440 | tf_op jit(solution)/shard_map/reduce_scatter | solution.py:49
  75.3 6.7 %copy-start.1 = (bf16[1,128,96,128]{3,2,1,0:T(8,128)(2,1)S(1)}, bf16[1,128,96,128]{3,2,1,0:T(8,128)(2,1)}, u32[]{:S(2)}) copy-start(bf16[1,128,96,128]{3,2,1,0:T(8,128)(2,1)} %get-tuple-element.4) | copy-start | bytes 9437188
  75.3 6.7 %copy-start.2 = (bf16[1,128,96,128]{3,2,1,0:T(8,128)(2,1)S(1)}, bf16[1,128,96,128]{3,2,1,0:T(8,128)(2,1)}, u32[]{:S(2)}) copy-start(bf16[1,128,96,128]{3,2,1,0:T(8,128)(2,1)} %get-tuple-element.5) | copy-start | bytes 9437188
  85.6 3.2 %copy-start = (f32[128,32,128,1]{2,1,3,0:T(8,128)S(1)}, f32[128,32,128,1]{2,1,3,0:T(8,128)}, u32[]{:S(2)}) copy-start(f32[128,32,128,1]{2,1,3,0:T(8,128)} %fusion.4) | copy-start | bytes 6291460
  90.6 2.7 %copy-start.3 = (f32[128,32,128,1]{0,2,1,3:T(8,128)S(1)}, f32[128,32,128,1]{0,2,1,3:T(8,128)}, u32[]{:S(2)}) copy-start(f32[128,32,128,1]{0,2,1,3:T(8,128)} %copy.14) | copy-start | bytes 6291460
  93.3 2.4 %copy-start.5 = (s32[8,128,2]{1,2,0:T(2,128)S(1)}, s32[8,128,2]{1,2,0:T(2,128)}, u32[]{:S(2)}) copy-start(s32[8,128,2]{1,2,0:T(2,128)} %param.7) | copy-start | bytes 24580
Sparse Core Ops, SparseCore 0:
  24.9 46.9 all-gather.2
  95.8 30.2 reduce-scatter.1

commit v2 on v1

v2 whole, which is shorter than its diff:
```python
import functools
import math

import jax
import jax.numpy as jnp
import numpy as np
from jax import lax
from jax.experimental import pallas as pl
from jax.experimental.pallas import tpu as pltpu
from jax.sharding import PartitionSpec as P

L = 128
CHUNKS = 4
MESH = pl.DeviceIdType.MESH
BF = jnp.bfloat16
F32 = jnp.float32
NT = (((1,), (1,)), ((), ()))


def lag_table(bins, per, lags):
    phase = (np.arange(1, bins + 1)[:, None] * (np.arange(lags) - lags // 2)[None, :]) % (2 * bins)
    angle = phase.astype(np.float32) * np.float32(2.0 * math.pi / (2 * bins))
    both = np.stack([np.cos(angle), -np.sin(angle)]).astype(BF).astype(np.float32)
    table = np.einsum("pft,su->stpfu", both, np.eye(per, dtype=np.float32))
    return table.reshape(per * lags, 2 * bins * per).astype(BF)


def kernel(n, sources_ref, low_ref, high_ref, spectra_ref, valid_ref, table_ref, lag_ref, peak_ref,
           white, own_valid, table, picks, cross, part, from_core, from_x, to_x,
           load_sem, valid_sem, table_sem, send_sem, near_sem, pass_sem, recv_sem, red_send, red_recv):
    _, bins, rows, chans = white.shape
    per = sources_ref.shape[0]
    half = n // 2
    step = bins // CHUNKS
    group = n // 4
    fi = lax.axis_index("freq")
    r = lax.axis_index("rcv")
    x_idx, core = fi // 2, lax.rem(fi, 2)
    near = r + 1 - 2 * lax.rem(r, 2)
    peers = [lax.rem(r + 2 * d, n) for d in range(1, half)]
    core_dev = fi + 1 - 2 * core
    x_dev = lax.rem(fi + 2, 4)

    barrier = pltpu.get_barrier_semaphore()
    for dev in [(fi, near)] + [(fi, p) for p in peers] + [(core_dev, r), (x_dev, r)]:
        pl.semaphore_signal(barrier, inc=1, device_id=dev, device_id_type=MESH)

    def load(k):
        part_f = pl.ds(k * step, step)
        return pltpu.make_async_copy(spectra_ref.at[:, part_f], white.at[:, part_f], load_sem.at[k])

    for k in range(CHUNKS):
        load(k).start()
    valid_copy = pltpu.make_async_copy(valid_ref.at[pl.ds(fi * rows, rows)], own_valid, valid_sem)
    valid_copy.start()
    table_copy = pltpu.make_async_copy(table_ref, table, table_sem)
    table_copy.start()

    total = jnp.zeros((rows, chans), F32)
    for k in range(CHUNKS):
        load(k).wait()

        def add(i, acc, k=k):
            for u in range(4):
                f = k * step + i * 4 + u
                a = white[0, f].astype(F32)
                b = white[1, f].astype(F32)
                acc = acc + (a * a + b * b)
            return acc

        total = lax.fori_loop(0, step // 4, add, total)
    valid_copy.wait()
    valid_f = own_valid[...].astype(F32)
    scale = valid_f / jnp.sqrt(total * (1.0 / bins) + 1e-6)
    valid_w = jnp.concatenate([valid_f, jnp.zeros((chans - rows, chans), F32)], axis=0).astype(BF)

    row_id = lax.broadcasted_iota(jnp.int32, (4 * per, chans), 0)
    lane_id = lax.broadcasted_iota(jnp.int32, (4 * per, chans), 1)
    hit = jnp.zeros((4 * per, chans), F32)
    for s in range(per):
        off = sources_ref[s] - r * chans
        hit = jnp.where((lax.rem(row_id, per) == s) & (lane_id == off), 1.0, hit)
    pick = jnp.concatenate(
        [jnp.where(row_id // per == u, hit, 0.0) for u in range(4)], axis=1).astype(BF)
    tile = 4 * per
    picks[r, 0:tile] = lax.dot_general(
        hit.astype(BF), valid_w, NT, preferred_element_type=F32).astype(BF)

    pairs = step // 8
    width = 3 * tile * pairs

    def span(k):
        return pl.ds(0, tile + width) if k == 0 else pl.ds(tile + k * width, width)

    def send(block, k, to, sem):
        return pltpu.make_async_remote_copy(
            src_ref=picks.at[block, span(k)], dst_ref=picks.at[block, span(k)],
            send_sem=sem, recv_sem=recv_sem.at[block, k],
            device_id=(fi, to), device_id_type=MESH)

    def forward(k):
        for d, p in enumerate(peers):
            send(p, k, near, pass_sem.at[d, k]).wait_recv()
            send(p, k, near, pass_sem.at[d, k]).start()

    rest = chans - rows
    for k in range(CHUNKS):
        def whiten(i, _, k=k):
            top, low = [], []
            for u in range(8):
                f = k * step + i * 8 + u
                re = (white[0, f].astype(F32) * scale).astype(BF)
                im = (white[1, f].astype(F32) * scale).astype(BF)
                white[0, f] = re
                white[1, f] = im
                top.append(jnp.concatenate([re, im[0:rest]], axis=0))
                low.append(im[rest:])
            first = jnp.concatenate(top[0:4], axis=1)
            second = jnp.concatenate(top[4:8], axis=1)
            third = jnp.concatenate(
                [jnp.concatenate(low[0:4], axis=1), jnp.concatenate(low[4:8], axis=1)], axis=0)
            base = pl.multiple_of(tile + k * width + i * (3 * tile), tile)
            for m, w in enumerate((first, second, third)):
                picks[r, pl.ds(base + m * tile, tile)] = lax.dot_general(
                    pick, w, NT, preferred_element_type=F32).astype(BF)
            return 0

        lax.fori_loop(0, pairs, whiten, 0)
        if k == 0:
            pl.semaphore_wait(barrier, half + 2)
        send(r, k, near, near_sem.at[k]).start()
        for d, p in enumerate(peers):
            send(r, k, p, send_sem.at[d, k]).start()
        if k >= 1:
            forward(k - 1)

    forward(CHUNKS - 1)
    band = lax.broadcasted_iota(jnp.int32, (n, tile, chans), 1) // per
    blank = jnp.zeros((2 * chans - 2 * rows, chans), BF)
    for k in range(CHUNKS):
        send(near, k, near, near_sem.at[k]).wait_recv()
        for p in peers:
            other = p + 1 - 2 * lax.rem(p, 2)
            send(other, k, near, near_sem.at[k]).wait_recv()

        def correlate(i, _, k=k):
            base = pl.multiple_of(tile + k * width + i * (3 * tile), tile)
            shared = picks[:, pl.ds(base + 2 * tile, tile)].reshape(n * tile, chans)
            for q in range(2):
                lead = picks[:, pl.ds(base + q * tile, tile)].reshape(n * tile, chans)
                lhs = jnp.concatenate([lead, shared], axis=1)
                out_re = out_im = None
                for u in range(4):
                    f = k * step + i * 8 + q * 4 + u
                    re = white[0, f]
                    im = white[1, f]
                    neg = -re
                    if q == 0:
                        left = jnp.concatenate([re, im, blank], axis=0)
                        right = jnp.concatenate([im, neg, blank], axis=0)
                    else:
                        left = jnp.concatenate([re, im[0:rest], blank, im[rest:]], axis=0)
                        right = jnp.concatenate([im, neg[0:rest], blank, neg[rest:]], axis=0)
                    out = jnp.dot(lhs, jnp.concatenate([left, right], axis=1),
                                  preferred_element_type=F32)
                    one = out[:, 0:chans].reshape(n, tile, chans)
                    two = out[:, chans:].reshape(n, tile, chans)
                    out_re = one if u == 0 else jnp.where(band == u, one, out_re)
                    out_im = two if u == 0 else jnp.where(band == u, two, out_im)
                at = pl.multiple_of((k * step + i * 8 + q * 4) * per, tile)
                cross[:, pl.ds(at, tile)] = out_re.astype(BF)
                cross[:, pl.ds(bins * per + at, tile)] = out_im.astype(BF)
            return 0

        lax.fori_loop(0, pairs, correlate, 0)

    counts = jnp.dot(picks[:, 0:tile].reshape(n * tile, chans), valid_w, preferred_element_type=F32)
    body = per * L
    part[:, body:body + tile] = counts.reshape(n, tile, chans).astype(BF)
    table_copy.wait()

    def transform(i):
        def one(j, _):
            at = i * group + j
            part[at, 0:body] = jnp.dot(
                table[...], cross[at], preferred_element_type=F32).astype(BF)
            return 0

        lax.fori_loop(0, group, one, 0)

    def to_core(i, slot):
        return pltpu.make_async_remote_copy(
            src_ref=part.at[pl.ds(i * group, group)], dst_ref=from_core.at[slot],
            send_sem=red_send.at[slot], recv_sem=red_recv.at[slot],
            device_id=(core_dev, r), device_id_type=MESH)

    far_other = 2 * (1 - x_idx) + (1 - core)
    far_same = 2 * (1 - x_idx) + core
    transform(far_other)
    to_core(far_other, 0).start()
    transform(far_same)
    to_core(far_other, 0).wait_recv()

    def join(j, _):
        to_x[j] = (part[far_same * group + j].astype(F32) + from_core[0, j].astype(F32)).astype(BF)
        return 0

    lax.fori_loop(0, group, join, 0)
    cross_x = pltpu.make_async_remote_copy(
        src_ref=to_x, dst_ref=from_x, send_sem=red_send.at[2], recv_sem=red_recv.at[2],
        device_id=(x_dev, r), device_id_type=MESH)
    cross_x.start()
    transform(core_dev)
    to_core(core_dev, 1).start()
    transform(fi)
    to_core(core_dev, 1).wait_recv()
    cross_x.wait_recv()

    lag_id = lax.broadcasted_iota(jnp.int32, (L, chans), 0)

    def finish(j, _):
        def added(a, b):
            return (part[fi * group + j, a:b].astype(F32) + from_core[1, j, a:b].astype(F32)
                    + from_x[j, a:b].astype(F32))

        count = added(body, body + tile)
        for s in range(per):
            lag = added(s * L, s * L + L) / count[s:s + 1]
            lag = lag.astype(BF).astype(F32)
            row = j * per + s
            low = low_ref[pl.ds(row, 1), :]
            high = high_ref[pl.ds(row, 1), :]
            inside = (lag_id >= low) & (lag_id < high)
            peak_ref[pl.ds(row, 1), :] = jnp.max(
                jnp.where(inside, lag, -jnp.inf), axis=0, keepdims=True)
            lag_ref[row] = lag.T.astype(BF)
        return 0

    lax.fori_loop(0, group, finish, 0)

    for k in range(CHUNKS):
        send(r, k, near, near_sem.at[k]).wait_send()
        for d, p in enumerate(peers):
            send(r, k, p, send_sem.at[d, k]).wait_send()
            send(p, k, near, pass_sem.at[d, k]).wait_send()
    to_core(far_other, 0).wait_send()
    to_core(core_dev, 1).wait_send()
    cross_x.wait_send()


def local(n, spectra, valid, sources, bounds):
    _, bins, rows, chans = spectra.shape
    per = sources.shape[0]
    group = n // 4
    count = bounds.shape[0]
    table = jnp.asarray(lag_table(bins, per, L))
    span = per * L + 4 * per
    vmem = pl.BlockSpec(memory_space=pltpu.VMEM)
    hbm = pl.BlockSpec(memory_space=pl.ANY)
    dma = pltpu.SemaphoreType.DMA
    half = n // 2
    return pl.pallas_call(
        functools.partial(kernel, n),
        out_shape=(jax.ShapeDtypeStruct((count, chans, L), BF),
                   jax.ShapeDtypeStruct((count, chans), F32)),
        in_specs=[pl.BlockSpec(memory_space=pltpu.SMEM), vmem, vmem, hbm, hbm, hbm],
        out_specs=(vmem, vmem),
        scratch_shapes=[
            pltpu.VMEM((2, bins, rows, chans), BF),
            pltpu.VMEM((rows, chans), jnp.int32),
            pltpu.VMEM(table.shape, BF),
            pltpu.VMEM((n, 4 * per + bins // 8 * 12 * per, chans), BF),
            pltpu.VMEM((n, 2 * bins * per, chans), BF),
            pltpu.VMEM((n, span, chans), BF),
            pltpu.VMEM((2, group, span, chans), BF),
            pltpu.VMEM((group, span, chans), BF),
            pltpu.VMEM((group, span, chans), BF),
            dma((CHUNKS,)), dma, dma,
            dma((half, CHUNKS)), dma((CHUNKS,)), dma((half, CHUNKS)), dma((n, CHUNKS)),
            dma((3,)), dma((3,)),
        ],
        compiler_params=pltpu.CompilerParams(
            collective_id=0, has_side_effects=True, vmem_limit_bytes=60 * 1024 * 1024),
    )(sources, bounds[:, :, 0], bounds[:, :, 1], spectra, valid, table)


def solution(mesh):
    in_specs = (P(None, None, "freq", "rcv"), P(None, "rcv"), P("rcv"), P("freq", "rcv", None))
    out_specs = (P("freq", "rcv", None), P("freq", "rcv"))
    return jax.shard_map(functools.partial(local, mesh.shape["rcv"]), mesh=mesh,
                         in_specs=in_specs, out_specs=out_specs, check_vma=False)
```

time: 136 us -> 50 us (0.37)
  Pallas kernels: 0 us -> 44.3 us
  waiting for transfers between devices: 38.5 us -> 0 us
  blocking collectives: 32.4 us -> 0 us
  other arithmetic: 21 us -> 0 us
  matrix products: 20.2 us -> 0 us
  between operations: 14.2 us -> 0.64 us
  local copies, waits for them, and re-layouts: 9.22 us -> 4.32 us
    pallas_call x0 -> x1, Pallas kernels: none -> 44.3 us  [local(): pl.pallas_call(functools.partial(kernel, n), out_shape=(jax.ShapeDtypeStr...]
    all_gather x1 -> x0, blocking collectives: 32.4 us -> none  [local(): source_valid = lax.all_gather(picked_valid, 'rcv', axis=0, tiled=True)]
    reduce_scatter x1 -> x0, waiting for transfers between devices: 30.3 us -> none  [local(): lag_sum = lax.psum_scatter(partial, 'freq', scatter_dimension=0, tiled=True)]
    dot_general x7 -> x0, matrix products: 20.2 us -> none  [the longest x1 6.66 us: local(): jnp.einsum('fspw,pfwc->fsc', source_part, whitened, preferred_element_typ...]
    convert_element_type x2 -> x0, other arithmetic: 11.2 us -> none  [the longest x1 6.68 us: local(): whitened = (spectra_f * scaling).astype(jnp.bfloat16)]
    all_gather x1 -> x0, waiting for transfers between devices: 8.16 us -> none  [local(): source_part = lax.all_gather(picked, 'rcv', axis=1, tiled=True)]
    slice x1 -> x0, other arithmetic: 6.13 us -> none  [local(): swapped = jnp.stack([whitened[1], -whitened[0]], axis=0)]
    dot_general x2 -> x0, local copies, waits for them, and re-layouts: 5.04 us -> none  [the longest x1 3.17 us: local(): jnp.einsum('fspw,pfwc->fsc', source_part, swapped, preferred_element_type...]
  transfers between devices with their start and end apart: 2 -> 0, of which waited for: 2 -> 0; matrix products, arithmetic and copies ran while one was open for 5% -> 0% of each run, Pallas kernels for 0% -> 0%
where the time goes in v2:
time: 50 us; the launch traced here: 49.3 us
  Pallas kernels  44.3 us (89%)
  local copies, waits for them, and re-layouts  4.32 us (9%)
  between operations  0.64 us (1%)
    pallas_call x1, Pallas kernels, local(): pl.pallas_call(functools.partial(kernel, n), out_shape=(jax.ShapeDtypeStr...  44.3 us
    unnamed x2, local copies, waits for them, and re-layouts  2.95 us
    slice x1, local copies, waits for them, and re-layouts, local(): bounds[:, :, 1]  1.38 us

profile of v2, /device:TPU:0, one launch (start us, length us, event | category | flops | bytes accessed | tf_op | source)
XLA Modules:
  0.0 49.3 jit_solution(3869256793885273068)
XLA Ops:
  0.6 1.4 %fusion = (s32[8,128,1]{1,2,0:T(1,128)}, s32[8,128,1]{1,2,0:T(1,128)}) fusion(s32[8,128,2]{1,2,0:T(2,128)} %param.8), kind=kLoop, calls=%fused_computation | loop fusion | bytes 16384 | tf_op jit(solution)/shard_map/slice | solution.py:284
  2.0 44.3 %shard_map.68 = (bf16[8,128,128]{2,1,0:T(8,128)(2,1)}, f32[8,128]{1,0:T(8,128)}) custom-call(s32[4]{0:T(128)} %sources_ref.1, s32[8,128]{1,0:T(8,128)} %bitcast.7, s32[8,128]{1,0:T(8,128)} %bitcast.6, bf16[2,128,96,128]{3,2,1,0:T(8,128)(2,1)} %spectra_ref.1, s32[384,128]{1,0:T(8,128)} %valid_ref.1, bf16[512,1024]{1,0:T(8,128)(2,1)} %constant.2.clone.table_ref), custom_call_target="tpu_custom_call" | custom-call | tf_op jit(solution)/shard_map/pallas_call | solution.py:262
  46.3 1.7 %copy.13 = bf16[8,128,128]{2,1,0:T(8,128)(2,1)} copy(bf16[8,128,128]{2,1,0:T(8,128)(2,1)} %get-tuple-element.6) | data formatting | bytes 524288
  48.0 1.3 %copy.14 = f32[8,128]{1,0:T(8,128)} copy(f32[8,128]{1,0:T(8,128)} %get-tuple-element.7) | data formatting | bytes 8192

commit v3 on v2

v3 whole, which is shorter than its diff:
```python
import functools
import math

import jax
import jax.numpy as jnp
import numpy as np
from jax import lax
from jax.experimental import pallas as pl
from jax.experimental.pallas import tpu as pltpu
from jax.sharding import PartitionSpec as P

L = 128
CHUNKS = 8
EARLY = 2
MESH = pl.DeviceIdType.MESH
BF = jnp.bfloat16
F32 = jnp.float32
NT = (((1,), (1,)), ((), ()))


def lag_table(bins, per, lags):
    phase = (np.arange(1, bins + 1)[:, None] * (np.arange(lags) - lags // 2)[None, :]) % (2 * bins)
    angle = phase.astype(np.float32) * np.float32(2.0 * math.pi / (2 * bins))
    both = np.stack([np.cos(angle), -np.sin(angle)]).astype(BF).astype(np.float32)
    table = np.einsum("pft,su->stpfu", both, np.eye(per, dtype=np.float32))
    return table.reshape(per * lags, 2 * bins * per).astype(BF)


def kernel(n, sources_ref, spectra_ref, valid_ref, table_ref, total_ref,
           white, own_valid, table, picks, scales, cross, part, from_core, from_x, to_x,
           load_sem, valid_sem, table_sem, send_sem, near_sem, pass_sem, recv_sem, red_send, red_recv):
    _, bins, rows, chans = white.shape
    per = sources_ref.shape[0]
    half = n // 2
    step = bins // CHUNKS
    group = n // 4
    piece = group // 2
    fi = lax.axis_index("freq")
    r = lax.axis_index("rcv")
    x_idx, core = fi // 2, lax.rem(fi, 2)
    near = r + 1 - 2 * lax.rem(r, 2)
    peers = [lax.rem(r + 2 * d, n) for d in range(1, half)]
    core_dev = fi + 1 - 2 * core
    x_dev = lax.rem(fi + 2, 4)

    barrier = pltpu.get_barrier_semaphore()
    for dev in [(fi, near)] + [(fi, p) for p in peers] + [(core_dev, r), (x_dev, r)]:
        pl.semaphore_signal(barrier, inc=1, device_id=dev, device_id_type=MESH)

    def load(k):
        part_f = pl.ds(k * step, step)
        return pltpu.make_async_copy(spectra_ref.at[:, part_f], white.at[:, part_f], load_sem.at[k])

    for k in range(CHUNKS):
        load(k).start()
    valid_copy = pltpu.make_async_copy(valid_ref.at[pl.ds(fi * rows, rows)], own_valid, valid_sem)
    valid_copy.start()
    table_copy = pltpu.make_async_copy(table_ref, table, table_sem)
    table_copy.start()

    row_id = lax.broadcasted_iota(jnp.int32, (4 * per, chans), 0)
    lane_id = lax.broadcasted_iota(jnp.int32, (4 * per, chans), 1)
    hit = jnp.zeros((4 * per, chans), F32)
    for s in range(per):
        off = sources_ref[s] - r * chans
        hit = jnp.where((lax.rem(row_id, per) == s) & (lane_id == off), 1.0, hit)
    pick = jnp.concatenate(
        [jnp.where(row_id // per == u, hit, 0.0) for u in range(4)], axis=1).astype(BF)
    hit = hit.astype(BF)
    tile = 4 * per
    pairs = step // 8
    width = 3 * tile * pairs
    rest = chans - rows

    def send(block, k, to, sem):
        ref = scales.at[block] if k == CHUNKS else picks.at[block, pl.ds(k * width, width)]
        return pltpu.make_async_remote_copy(
            src_ref=ref, dst_ref=ref, send_sem=sem, recv_sem=recv_sem.at[block, k],
            device_id=(fi, to), device_id_type=MESH)

    def send_own(k):
        send(r, k, near, near_sem.at[k]).start()
        for d, p in enumerate(peers):
            send(r, k, p, send_sem.at[d, k]).start()

    def forward(k):
        for d, p in enumerate(peers):
            send(p, k, near, pass_sem.at[d, k]).wait_recv()
            send(p, k, near, pass_sem.at[d, k]).start()

    def arrive(k):
        send(near, k, near, near_sem.at[k]).wait_recv()
        for p in peers:
            other = p + 1 - 2 * lax.rem(p, 2)
            send(other, k, near, near_sem.at[k]).wait_recv()

    def choose(k):
        def one(i, _):
            top, low = [], []
            for u in range(8):
                f = k * step + i * 8 + u
                im = white[1, f]
                top.append(jnp.concatenate([white[0, f], im[0:rest]], axis=0))
                low.append(im[rest:])
            first = jnp.concatenate(top[0:4], axis=1)
            second = jnp.concatenate(top[4:8], axis=1)
            third = jnp.concatenate(
                [jnp.concatenate(low[0:4], axis=1), jnp.concatenate(low[4:8], axis=1)], axis=0)
            base = pl.multiple_of(k * width + i * (3 * tile), tile)
            for m, w in enumerate((first, second, third)):
                picks[r, pl.ds(base + m * tile, tile)] = lax.dot_general(
                    pick, w, NT, preferred_element_type=F32).astype(BF)
            return 0

        lax.fori_loop(0, pairs, one, 0)

    for k in range(EARLY):
        load(k).wait()
        choose(k)
        if k == 0:
            pl.semaphore_wait(barrier, half + 2)
        send_own(k)

    total = jnp.zeros((rows, chans), F32)
    for k in range(CHUNKS):
        if k >= EARLY:
            load(k).wait()

        def add(i, acc, k=k):
            for u in range(4):
                f = k * step + i * 4 + u
                a = white[0, f].astype(F32)
                b = white[1, f].astype(F32)
                acc = acc + (a * a + b * b)
            return acc

        total = lax.fori_loop(0, step // 4, add, total)
    valid_copy.wait()
    valid_f = own_valid[...].astype(F32)
    scale = valid_f / jnp.sqrt(total * (1.0 / bins) + 1e-6)
    valid_w = jnp.concatenate([valid_f, jnp.zeros((chans - rows, chans), F32)], axis=0).astype(BF)
    left_over = jnp.concatenate([scale, scale[0:rest], scale[rest:], scale[rest:]], axis=0)
    chosen = jnp.zeros((tile, 2 * chans), F32)
    for _ in range(3):
        high = left_over.astype(BF)
        left_over = left_over - high.astype(F32)
        chosen = chosen + lax.dot_general(hit, high, NT, preferred_element_type=F32)
    scales[r] = chosen
    send_own(CHUNKS)

    for k in range(EARLY, CHUNKS):
        choose(k)
        send_own(k)
        forward(k - EARLY)
        if k == EARLY:
            forward(CHUNKS)

    band = lax.broadcasted_iota(jnp.int32, (n, tile, chans), 1) // per
    blank = jnp.zeros((2 * chans - 2 * rows, chans), BF)

    def correlate(k):
        def one(i, _):
            base = pl.multiple_of(k * width + i * (3 * tile), tile)

            def sources_of(m, lanes):
                raw = picks[:, pl.ds(base + m * tile, tile)].astype(F32)
                return (raw * scales[:, :, lanes]).astype(BF).reshape(n * tile, chans)

            shared = sources_of(2, slice(chans, 2 * chans))
            for q in range(2):
                lhs = jnp.concatenate([sources_of(q, slice(0, chans)), shared], axis=1)
                out_re = out_im = None
                for u in range(4):
                    f = k * step + i * 8 + q * 4 + u
                    re = (white[0, f].astype(F32) * scale).astype(BF)
                    im = (white[1, f].astype(F32) * scale).astype(BF)
                    neg = -re
                    if q == 0:
                        left = jnp.concatenate([re, im, blank], axis=0)
                        right = jnp.concatenate([im, neg, blank], axis=0)
                    else:
                        left = jnp.concatenate([re, im[0:rest], blank, im[rest:]], axis=0)
                        right = jnp.concatenate([im, neg[0:rest], blank, neg[rest:]], axis=0)
                    out = jnp.dot(lhs, jnp.concatenate([left, right], axis=1),
                                  preferred_element_type=F32)
                    first = out[:, 0:chans].reshape(n, tile, chans)
                    second = out[:, chans:].reshape(n, tile, chans)
                    out_re = first if u == 0 else jnp.where(band == u, first, out_re)
                    out_im = second if u == 0 else jnp.where(band == u, second, out_im)
                at = pl.multiple_of((k * step + i * 8 + q * 4) * per, tile)
                cross[:, pl.ds(at, tile)] = out_re.astype(BF)
                cross[:, pl.ds(bins * per + at, tile)] = out_im.astype(BF)
            return 0

        lax.fori_loop(0, pairs, one, 0)

    body = per * L
    for k in range(CHUNKS):
        if k + CHUNKS - EARLY < CHUNKS:
            forward(k + CHUNKS - EARLY)
        if k == 0:
            arrive(CHUNKS)
            usable = jnp.where(scales[:, :, 0:chans] > 0.0, 1.0, 0.0)
            counts = jnp.dot(usable.astype(BF).reshape(n * tile, chans), valid_w,
                             preferred_element_type=F32)
            part[:, body:body + tile] = counts.reshape(n, tile, chans).astype(BF)
        arrive(k)
        correlate(k)
    table_copy.wait()

    def transform(i, h):
        def one(j, _):
            at = i * group + h * piece + j
            part[at, 0:body] = jnp.dot(
                table[...], cross[at], preferred_element_type=F32).astype(BF)
            return 0

        lax.fori_loop(0, piece, one, 0)

    def to_core(i, slot, h):
        return pltpu.make_async_remote_copy(
            src_ref=part.at[pl.ds(i * group + h * piece, piece)],
            dst_ref=from_core.at[slot, pl.ds(h * piece, piece)],
            send_sem=red_send.at[slot, h], recv_sem=red_recv.at[slot, h],
            device_id=(core_dev, r), device_id_type=MESH)

    def over_x(h):
        mine = pl.ds(h * piece, piece)
        return pltpu.make_async_remote_copy(
            src_ref=to_x.at[mine], dst_ref=from_x.at[mine],
            send_sem=red_send.at[2, h], recv_sem=red_recv.at[2, h],
            device_id=(x_dev, r), device_id_type=MESH)

    far_other = 2 * (1 - x_idx) + (1 - core)
    far_same = 2 * (1 - x_idx) + core
    for h in range(2):
        transform(far_other, h)
        to_core(far_other, 0, h).start()
    for h in range(2):
        transform(far_same, h)
        to_core(far_other, 0, h).wait_recv()

        def join(j, _, h=h):
            at = h * piece + j
            to_x[at] = (part[far_same * group + at].astype(F32)
                        + from_core[0, at].astype(F32)).astype(BF)
            return 0

        lax.fori_loop(0, piece, join, 0)
        over_x(h).start()
    for h in range(2):
        transform(core_dev, h)
        to_core(core_dev, 1, h).start()
    for h in range(2):
        transform(fi, h)
    for h in range(2):
        to_core(core_dev, 1, h).wait_recv()
        over_x(h).wait_recv()

        def add_up(j, _, h=h):
            at = h * piece + j
            total_ref[at] = (part[fi * group + at].astype(F32) + from_core[1, at].astype(F32)
                             + from_x[at].astype(F32))
            return 0

        lax.fori_loop(0, piece, add_up, 0)

    for k in range(CHUNKS + 1):
        send(r, k, near, near_sem.at[k]).wait_send()
        for d, p in enumerate(peers):
            send(r, k, p, send_sem.at[d, k]).wait_send()
            send(p, k, near, pass_sem.at[d, k]).wait_send()
    for h in range(2):
        to_core(far_other, 0, h).wait_send()
        to_core(core_dev, 1, h).wait_send()
        over_x(h).wait_send()


def finish(per, total_ref, bounds_ref, lag_ref, peak_ref):
    group, _, chans = total_ref.shape
    lag_id = lax.broadcasted_iota(jnp.int32, (L, chans), 0)

    def one(j, _):
        count = total_ref[j, per * L:per * L + per]
        for s in range(per):
            lag = total_ref[j, s * L:s * L + L] / count[s:s + 1]
            lag = lag.astype(BF).astype(F32)
            row = j * per + s
            inside = (lag_id >= bounds_ref[row, 0:1]) & (lag_id < bounds_ref[row, 1:2])
            peak_ref[pl.ds(row, 1), :] = jnp.max(
                jnp.where(inside, lag, -jnp.inf), axis=0, keepdims=True)
            lag_ref[row] = lag.T.astype(BF)
        return 0

    lax.fori_loop(0, group, one, 0, unroll=group <= 2)


def local(n, spectra, valid, sources, bounds):
    _, bins, rows, chans = spectra.shape
    per = sources.shape[0]
    group = n // 4
    count = bounds.shape[0]
    table = jnp.asarray(lag_table(bins, per, L))
    span = per * L + 4 * per
    vmem = pl.BlockSpec(memory_space=pltpu.VMEM)
    hbm = pl.BlockSpec(memory_space=pl.ANY)
    dma = pltpu.SemaphoreType.DMA
    half = n // 2
    total = pl.pallas_call(
        functools.partial(kernel, n),
        out_shape=jax.ShapeDtypeStruct((group, span, chans), F32),
        in_specs=[pl.BlockSpec(memory_space=pltpu.SMEM), hbm, hbm, hbm],
        out_specs=vmem,
        scratch_shapes=[
            pltpu.VMEM((2, bins, rows, chans), BF),
            pltpu.VMEM((rows, chans), jnp.int32),
            pltpu.VMEM(table.shape, BF),
            pltpu.VMEM((n, bins // 8 * 12 * per, chans), BF),
            pltpu.VMEM((n, 4 * per, 2 * chans), F32),
            pltpu.VMEM((n, 2 * bins * per, chans), BF),
            pltpu.VMEM((n, span, chans), BF),
            pltpu.VMEM((2, group, span, chans), BF),
            pltpu.VMEM((group, span, chans), BF),
            pltpu.VMEM((group, span, chans), BF),
            dma((CHUNKS,)), dma, dma,
            dma((half, CHUNKS + 1)), dma((CHUNKS + 1,)), dma((half, CHUNKS + 1)),
            dma((n, CHUNKS + 1)), dma((3, 2)), dma((3, 2)),
        ],
        compiler_params=pltpu.CompilerParams(
            collective_id=0, has_side_effects=True, vmem_limit_bytes=62 * 1024 * 1024),
    )(sources, spectra, valid, table)
    return pl.pallas_call(
        functools.partial(finish, per),
        out_shape=(jax.ShapeDtypeStruct((count, chans, L), BF),
                   jax.ShapeDtypeStruct((count, chans), F32)),
        in_specs=[vmem, vmem],
        out_specs=(vmem, vmem),
        compiler_params=pltpu.CompilerParams(vmem_limit_bytes=32 * 1024 * 1024),
    )(total, bounds.transpose(0, 2, 1))


def solution(mesh):
    in_specs = (P(None, None, "freq", "rcv"), P(None, "rcv"), P("rcv"), P("freq", "rcv", None))
    out_specs = (P("freq", "rcv", None), P("freq", "rcv"))
    return jax.shard_map(functools.partial(local, mesh.shape["rcv"]), mesh=mesh,
                         in_specs=in_specs, out_specs=out_specs, check_vma=False)
```

time: 50 us -> 47 us (0.940); the launches traced: 49.3 us -> 46.8 us
  local copies, waits for them, and re-layouts: 4.32 us -> 1.04 us
  Pallas kernels: 44.3 us -> 45.1 us
    unnamed x2 -> x4, local copies, waits for them, and re-layouts: 2.95 us -> 1.04 us
    slice x1 -> x0, local copies, waits for them, and re-layouts: 1.38 us -> none  [local(): bounds[:, :, 1]]
    pallas_call x1 -> x2, Pallas kernels: 44.3 us -> 45.1 us  [the longest x1 44.2 us: local(): pl.pallas_call(functools.partial(kernel, n), out_shape=jax.ShapeDtypeStru...]
where the time goes in v3:
time: 47 us; the launch traced here: 46.8 us
  Pallas kernels  45.1 us (96%)
  local copies, waits for them, and re-layouts  1.04 us (2%)
  between operations  0.66 us (1%)
    pallas_call x1, Pallas kernels, local(): pl.pallas_call(functools.partial(kernel, n), out_shape=jax.ShapeDtypeStru...  44.2 us
    unnamed x4, local copies, waits for them, and re-layouts  1.04 us

profile of v3, /device:TPU:0, one launch (start us, length us, event | category | flops | bytes accessed | tf_op | source)
XLA Modules:
  0.0 46.8 jit_solution(6753624265211021925)
XLA Ops:
  0.6 0.0 copy-start.1
  0.6 44.2 %shard_map.68.total_ref = f32[2,528,128]{2,1,0:T(8,128)} custom-call(s32[4]{0:T(128)} %sources_ref.1, bf16[2,128,96,128]{3,2,1,0:T(8,128)(2,1)} %spectra_ref.1, s32[384,128]{1,0:T(8,128)} %valid_ref.1, bf16[512,1024]{1,0:T(8,128)(2,1)} %constant.2.clone.table_ref), custom_call_target="tpu_custom_call" | custom-call | tf_op jit(solution)/shard_map/pallas_call | solution.py:309
  44.8 0.0 copy-done.1
  44.8 0.0 copy-start
  44.8 1.0 %copy-done = f32[2,528,128]{2,1,0:T(8,128)S(1)} copy-done((f32[2,528,128]{2,1,0:T(8,128)S(1)}, f32[2,528,128]{2,1,0:T(8,128)}, u32[]{:S(2)}) %copy-start) | copy-done | bytes 540696
  45.9 0.9 %shard_map.69 = (bf16[8,128,128]{2,1,0:T(8,128)(2,1)}, f32[8,128]{1,0:T(8,128)}) custom-call(f32[2,528,128]{2,1,0:T(8,128)S(1)} %copy-done, s32[8,2,128]{2,1,0:T(2,128)S(1)} %bitcast.1), custom_call_target="tpu_custom_call" | custom-call | tf_op jit(solution)/shard_map/pallas_call | solution.py:332
Async XLA Ops:
  0.6 44.2 %copy-start.1 = (s32[8,128,2]{1,2,0:T(2,128)S(1)}, s32[8,128,2]{1,2,0:T(2,128)}, u32[]{:S(2)}) copy-start(s32[8,128,2]{1,2,0:T(2,128)} %param.8) | copy-start | bytes 24580
  44.8 1.0 %copy-start = (f32[2,528,128]{2,1,0:T(8,128)S(1)}, f32[2,528,128]{2,1,0:T(8,128)}, u32[]{:S(2)}) copy-start(f32[2,528,128]{2,1,0:T(8,128)} %shard_map.68.total_ref) | copy-start | bytes 1622020

commit v4 on v3

--- a/solution.py
+++ b/solution.py
@@ -27,7 +27,7 @@
 
 
 def kernel(n, sources_ref, spectra_ref, valid_ref, table_ref, total_ref,
-           white, own_valid, table, picks, scales, cross, part, from_core, from_x, to_x,
+           white, own_valid, table, onehot, picks, scales, cross, part, from_core, from_x, to_x,
            load_sem, valid_sem, table_sem, send_sem, near_sem, pass_sem, recv_sem, red_send, red_recv):
     _, bins, rows, chans = white.shape
     per = sources_ref.shape[0]
@@ -60,13 +60,17 @@
 
     row_id = lax.broadcasted_iota(jnp.int32, (4 * per, chans), 0)
     lane_id = lax.broadcasted_iota(jnp.int32, (4 * per, chans), 1)
+    chan_id = lax.broadcasted_iota(jnp.int32, (chans, chans), 0)
+    slot_id = lax.broadcasted_iota(jnp.int32, (chans, chans), 1)
     hit = jnp.zeros((4 * per, chans), F32)
+    place = jnp.zeros((chans, chans), F32)
     for s in range(per):
         off = sources_ref[s] - r * chans
         hit = jnp.where((lax.rem(row_id, per) == s) & (lane_id == off), 1.0, hit)
-    pick = jnp.concatenate(
-        [jnp.where(row_id // per == u, hit, 0.0) for u in range(4)], axis=1).astype(BF)
+        place = jnp.where((lax.rem(slot_id, per) == s) & (chan_id == off), 1.0, place)
     hit = hit.astype(BF)
+    for u in range(step):
+        onehot[u * chans:(u + 1) * chans] = jnp.where(slot_id // per == u, place, 0.0).astype(BF)
     tile = 4 * per
     pairs = step // 8
     width = 3 * tile * pairs
@@ -95,24 +99,20 @@
             send(other, k, near, near_sem.at[k]).wait_recv()
 
     def choose(k):
-        def one(i, _):
-            top, low = [], []
-            for u in range(8):
-                f = k * step + i * 8 + u
-                im = white[1, f]
-                top.append(jnp.concatenate([white[0, f], im[0:rest]], axis=0))
-                low.append(im[rest:])
-            first = jnp.concatenate(top[0:4], axis=1)
-            second = jnp.concatenate(top[4:8], axis=1)
-            third = jnp.concatenate(
-                [jnp.concatenate(low[0:4], axis=1), jnp.concatenate(low[4:8], axis=1)], axis=0)
-            base = pl.multiple_of(k * width + i * (3 * tile), tile)
-            for m, w in enumerate((first, second, third)):
-                picks[r, pl.ds(base + m * tile, tile)] = lax.dot_general(
-                    pick, w, NT, preferred_element_type=F32).astype(BF)
-            return 0
-
-        lax.fori_loop(0, pairs, one, 0)
+        lhs = jnp.concatenate(
+            [jnp.concatenate([white[0, k * step + u], white[1, k * step + u]], axis=0)
+             for u in range(step)], axis=1)
+        out = jnp.dot(lhs, onehot[...], preferred_element_type=F32)
+        lead = out[0:chans].T
+        tail = jnp.concatenate([out[chans:], out[chans:]], axis=0).T
+        for i in range(pairs):
+            base = k * width + i * 3 * tile
+            one = slice(2 * i * tile, (2 * i + 1) * tile)
+            two = slice((2 * i + 1) * tile, (2 * i + 2) * tile)
+            picks[r, base:base + tile] = lead[one].astype(BF)
+            picks[r, base + tile:base + 2 * tile] = lead[two].astype(BF)
+            picks[r, base + 2 * tile:base + 3 * tile] = jnp.where(
+                lane_id < chans // 2, tail[one], tail[two]).astype(BF)
 
     for k in range(EARLY):
         load(k).wait()
@@ -208,11 +208,13 @@
         correlate(k)
     table_copy.wait()
 
-    def transform(i, h):
+    def transform(i):
         def one(j, _):
-            at = i * group + h * piece + j
-            part[at, 0:body] = jnp.dot(
-                table[...], cross[at], preferred_element_type=F32).astype(BF)
+            at = i * group + 2 * j
+            both = jnp.dot(table[...], jnp.concatenate([cross[at], cross[at + 1]], axis=1),
+                           preferred_element_type=F32)
+            part[at, 0:body] = both[:, 0:chans].astype(BF)
+            part[at + 1, 0:body] = both[:, chans:].astype(BF)
             return 0
 
         lax.fori_loop(0, piece, one, 0)
@@ -233,11 +235,11 @@
 
     far_other = 2 * (1 - x_idx) + (1 - core)
     far_same = 2 * (1 - x_idx) + core
-    for h in range(2):
-        transform(far_other, h)
+    transform(far_other)
+    for h in range(2):
         to_core(far_other, 0, h).start()
-    for h in range(2):
-        transform(far_same, h)
+    transform(far_same)
+    for h in range(2):
         to_core(far_other, 0, h).wait_recv()
 
         def join(j, _, h=h):
@@ -248,11 +250,10 @@
 
         lax.fori_loop(0, piece, join, 0)
         over_x(h).start()
-    for h in range(2):
-        transform(core_dev, h)
+    transform(core_dev)
+    for h in range(2):
         to_core(core_dev, 1, h).start()
-    for h in range(2):
-        transform(fi, h)
+    transform(fi)
     for h in range(2):
         to_core(core_dev, 1, h).wait_recv()
         over_x(h).wait_recv()
@@ -315,6 +316,7 @@
             pltpu.VMEM((2, bins, rows, chans), BF),
             pltpu.VMEM((rows, chans), jnp.int32),
             pltpu.VMEM(table.shape, BF),
+            pltpu.VMEM((bins // CHUNKS * chans, chans), BF),
             pltpu.VMEM((n, bins // 8 * 12 * per, chans), BF),
             pltpu.VMEM((n, 4 * per, 2 * chans), F32),
             pltpu.VMEM((n, 2 * bins * per, chans), BF),

time: 47 us -> 47.2 us (level)
  no operation moved by 1% of the time
where the time goes in v4:
time: 47.2 us; the launch traced here: 47 us
  Pallas kernels  45.2 us (96%)
  local copies, waits for them, and re-layouts  1.04 us (2%)
  between operations  0.66 us (1%)
    pallas_call x1, Pallas kernels, local(): pl.pallas_call(functools.partial(kernel, n), out_shape=jax.ShapeDtypeStru...  44.3 us
    unnamed x4, local copies, waits for them, and re-layouts  1.04 us

profile of v4, /device:TPU:0, one launch (start us, length us, event | category | flops | bytes accessed | tf_op | source)
XLA Modules:
  0.0 47.0 jit_solution(6086242223020206035)
XLA Ops:
  0.6 0.0 copy-start.1
  0.6 44.3 %shard_map.68.total_ref = f32[2,528,128]{2,1,0:T(8,128)} custom-call(s32[4]{0:T(128)} %sources_ref.1, bf16[2,128,96,128]{3,2,1,0:T(8,128)(2,1)} %spectra_ref.1, s32[384,128]{1,0:T(8,128)} %valid_ref.1, bf16[512,1024]{1,0:T(8,128)(2,1)} %constant.2.clone.table_ref), custom_call_target="tpu_custom_call" | custom-call | tf_op jit(solution)/shard_map/pallas_call | solution.py:310
  45.0 0.0 copy-done.1
  45.0 0.0 copy-start
  45.0 1.0 %copy-done = f32[2,528,128]{2,1,0:T(8,128)S(1)} copy-done((f32[2,528,128]{2,1,0:T(8,128)S(1)}, f32[2,528,128]{2,1,0:T(8,128)}, u32[]{:S(2)}) %copy-start) | copy-done | bytes 540696
  46.0 0.9 %shard_map.69 = (bf16[8,128,128]{2,1,0:T(8,128)(2,1)}, f32[8,128]{1,0:T(8,128)}) custom-call(f32[2,528,128]{2,1,0:T(8,128)S(1)} %copy-done, s32[8,2,128]{2,1,0:T(2,128)S(1)} %bitcast.1), custom_call_target="tpu_custom_call" | custom-call | tf_op jit(solution)/shard_map/pallas_call | solution.py:334
Async XLA Ops:
  0.6 44.3 %copy-start.1 = (s32[8,128,2]{1,2,0:T(2,128)S(1)}, s32[8,128,2]{1,2,0:T(2,128)}, u32[]{:S(2)}) copy-start(s32[8,128,2]{1,2,0:T(2,128)} %param.8) | copy-start | bytes 24580
  45.0 1.0 %copy-start = (f32[2,528,128]{2,1,0:T(8,128)S(1)}, f32[2,528,128]{2,1,0:T(8,128)}, u32[]{:S(2)}) copy-start(f32[2,528,128]{2,1,0:T(8,128)} %shard_map.68.total_ref) | copy-start | bytes 1622020

commit v5 on v4

--- a/solution.py
+++ b/solution.py
@@ -11,7 +11,8 @@
 
 L = 128
 CHUNKS = 8
-EARLY = 2
+EARLY = 3
+AHEAD = 3
 MESH = pl.DeviceIdType.MESH
 BF = jnp.bfloat16
 F32 = jnp.float32
@@ -27,7 +28,7 @@
 
 
 def kernel(n, sources_ref, spectra_ref, valid_ref, table_ref, total_ref,
-           white, own_valid, table, onehot, picks, scales, cross, part, from_core, from_x, to_x,
+           white, own_valid, table, onehot, picks, scales, spread, cross, part, from_core, from_x, to_x,
            load_sem, valid_sem, table_sem, send_sem, near_sem, pass_sem, recv_sem, red_send, red_recv):
     _, bins, rows, chans = white.shape
     per = sources_ref.shape[0]
@@ -39,7 +40,17 @@
     r = lax.axis_index("rcv")
     x_idx, core = fi // 2, lax.rem(fi, 2)
     near = r + 1 - 2 * lax.rem(r, 2)
-    peers = [lax.rem(r + 2 * d, n) for d in range(1, half)]
+    first_block = r // group
+    blocks = [lax.rem(first_block + o, 4) for o in range(4)]
+
+    def column(o):
+        inner = lax.rem(r, group) // 2
+        return [blocks[o] * group + 2 * lax.rem(inner + t, piece) + lax.rem(r, 2)
+                for t in range(piece) if (o, t) != (0, 0)]
+
+    halves = [column(0) + column(2), column(1) + column(3)]
+    peers = halves[0] + halves[1]
+    ranges = [range(len(halves[0])), range(len(halves[0]), len(peers))]
     core_dev = fi + 1 - 2 * core
     x_dev = lax.rem(fi + 2, 4)
 
@@ -82,19 +93,21 @@
             src_ref=ref, dst_ref=ref, send_sem=sem, recv_sem=recv_sem.at[block, k],
             device_id=(fi, to), device_id_type=MESH)
 
-    def send_own(k):
-        send(r, k, near, near_sem.at[k]).start()
-        for d, p in enumerate(peers):
-            send(r, k, p, send_sem.at[d, k]).start()
-
-    def forward(k):
-        for d, p in enumerate(peers):
-            send(p, k, near, pass_sem.at[d, k]).wait_recv()
-            send(p, k, near, pass_sem.at[d, k]).start()
-
-    def arrive(k):
-        send(near, k, near, near_sem.at[k]).wait_recv()
-        for p in peers:
+    def send_own(k, g):
+        if g == 0:
+            send(r, k, near, near_sem.at[k]).start()
+        for d in ranges[g]:
+            send(r, k, peers[d], send_sem.at[d, k]).start()
+
+    def forward(k, g):
+        for d in ranges[g]:
+            send(peers[d], k, near, pass_sem.at[d, k]).wait_recv()
+            send(peers[d], k, near, pass_sem.at[d, k]).start()
+
+    def arrive(k, g):
+        if g == 0:
+            send(near, k, near, near_sem.at[k]).wait_recv()
+        for p in halves[g]:
             other = p + 1 - 2 * lax.rem(p, 2)
             send(other, k, near, near_sem.at[k]).wait_recv()
 
@@ -119,7 +132,7 @@
         choose(k)
         if k == 0:
             pl.semaphore_wait(barrier, half + 2)
-        send_own(k)
+        send_own(k, 0)
 
     total = jnp.zeros((rows, chans), F32)
     for k in range(CHUNKS):
@@ -139,36 +152,44 @@
     valid_f = own_valid[...].astype(F32)
     scale = valid_f / jnp.sqrt(total * (1.0 / bins) + 1e-6)
     valid_w = jnp.concatenate([valid_f, jnp.zeros((chans - rows, chans), F32)], axis=0).astype(BF)
-    left_over = jnp.concatenate([scale, scale[0:rest], scale[rest:], scale[rest:]], axis=0)
-    chosen = jnp.zeros((tile, 2 * chans), F32)
+    left_over = jnp.concatenate([scale, scale[0:rest]], axis=0)
+    chosen = jnp.zeros((tile, chans), F32)
     for _ in range(3):
         high = left_over.astype(BF)
         left_over = left_over - high.astype(F32)
         chosen = chosen + lax.dot_general(hit, high, NT, preferred_element_type=F32)
-    scales[r] = chosen
-    send_own(CHUNKS)
+    scales[r] = chosen[0:2 * per]
+    send_own(CHUNKS, 0)
+    send_own(CHUNKS, 1)
 
     for k in range(EARLY, CHUNKS):
         choose(k)
-        send_own(k)
-        forward(k - EARLY)
-        if k == EARLY:
-            forward(CHUNKS)
-
-    band = lax.broadcasted_iota(jnp.int32, (n, tile, chans), 1) // per
+        send_own(k, 0)
+    for k in range(CHUNKS):
+        send_own(k, 1)
+    order = [(k, g) for g in range(2) for k in range(CHUNKS)]
+    for k, g in order[:AHEAD]:
+        forward(k, g)
+    forward(CHUNKS, 0)
+    forward(CHUNKS, 1)
+
+    band = lax.broadcasted_iota(jnp.int32, (half, tile, chans), 1) // per
     blank = jnp.zeros((2 * chans - 2 * rows, chans), BF)
 
-    def correlate(k):
+    def correlate(k, g):
+        owned = [pl.ds(blocks[g + o] * group, group) for o in (0, 2)]
+
         def one(i, _):
             base = pl.multiple_of(k * width + i * (3 * tile), tile)
 
-            def sources_of(m, lanes):
-                raw = picks[:, pl.ds(base + m * tile, tile)].astype(F32)
-                return (raw * scales[:, :, lanes]).astype(BF).reshape(n * tile, chans)
-
-            shared = sources_of(2, slice(chans, 2 * chans))
+            def sources_of(at, m):
+                return jnp.concatenate([
+                    (picks[o, pl.ds(base + at * tile, tile)].astype(F32) * spread[m, o]).astype(BF)
+                    for o in owned], axis=0).reshape(half * tile, chans)
+
+            shared = sources_of(2, 1)
             for q in range(2):
-                lhs = jnp.concatenate([sources_of(q, slice(0, chans)), shared], axis=1)
+                lhs = jnp.concatenate([sources_of(q, 0), shared], axis=1)
                 out_re = out_im = None
                 for u in range(4):
                     f = k * step + i * 8 + q * 4 + u
@@ -183,30 +204,32 @@
                         right = jnp.concatenate([im, neg[0:rest], blank, neg[rest:]], axis=0)
                     out = jnp.dot(lhs, jnp.concatenate([left, right], axis=1),
                                   preferred_element_type=F32)
-                    first = out[:, 0:chans].reshape(n, tile, chans)
-                    second = out[:, chans:].reshape(n, tile, chans)
+                    first = out[:, 0:chans].reshape(half, tile, chans)
+                    second = out[:, chans:].reshape(half, tile, chans)
                     out_re = first if u == 0 else jnp.where(band == u, first, out_re)
                     out_im = second if u == 0 else jnp.where(band == u, second, out_im)
                 at = pl.multiple_of((k * step + i * 8 + q * 4) * per, tile)
-                cross[:, pl.ds(at, tile)] = out_re.astype(BF)
-                cross[:, pl.ds(bins * per + at, tile)] = out_im.astype(BF)
+                for m, o in enumerate(owned):
+                    mine = slice(m * group, (m + 1) * group)
+                    cross[o, pl.ds(at, tile)] = out_re[mine].astype(BF)
+                    cross[o, pl.ds(bins * per + at, tile)] = out_im[mine].astype(BF)
             return 0
 
         lax.fori_loop(0, pairs, one, 0)
 
     body = per * L
-    for k in range(CHUNKS):
-        if k + CHUNKS - EARLY < CHUNKS:
-            forward(k + CHUNKS - EARLY)
-        if k == 0:
-            arrive(CHUNKS)
-            usable = jnp.where(scales[:, :, 0:chans] > 0.0, 1.0, 0.0)
-            counts = jnp.dot(usable.astype(BF).reshape(n * tile, chans), valid_w,
-                             preferred_element_type=F32)
-            part[:, body:body + tile] = counts.reshape(n, tile, chans).astype(BF)
-        arrive(k)
-        correlate(k)
-    table_copy.wait()
+    arrive(CHUNKS, 0)
+    arrive(CHUNKS, 1)
+    every = scales[...].reshape(n * 2 * per, chans)
+    lane = lax.broadcasted_iota(jnp.int32, every.shape, 1)
+    low = jnp.where(lane < chans // 2, pltpu.roll(every, rows, 1), pltpu.roll(every, rest, 1))
+    for m, src in enumerate((every, low)):
+        src = src.reshape(n, 2 * per, chans)
+        spread[m] = jnp.concatenate([src, src], axis=1)
+    usable = jnp.where(spread[0] > 0.0, 1.0, 0.0)
+    counts = jnp.dot(usable.astype(BF).reshape(n * tile, chans), valid_w,
+                     preferred_element_type=F32)
+    part[:, body:body + tile] = counts.reshape(n, tile, chans).astype(BF)
 
     def transform(i):
         def one(j, _):
@@ -235,25 +258,41 @@
 
     far_other = 2 * (1 - x_idx) + (1 - core)
     far_same = 2 * (1 - x_idx) + core
-    transform(far_other)
-    for h in range(2):
-        to_core(far_other, 0, h).start()
-    transform(far_same)
-    for h in range(2):
-        to_core(far_other, 0, h).wait_recv()
-
-        def join(j, _, h=h):
-            at = h * piece + j
-            to_x[at] = (part[far_same * group + at].astype(F32)
-                        + from_core[0, at].astype(F32)).astype(BF)
-            return 0
-
-        lax.fori_loop(0, piece, join, 0)
-        over_x(h).start()
-    transform(core_dev)
-    for h in range(2):
-        to_core(core_dev, 1, h).start()
-    transform(fi)
+
+    def gather_sums():
+        transform(far_same)
+        for h in range(2):
+            to_core(far_other, 0, h).wait_recv()
+
+            def join(j, _, h=h):
+                at = h * piece + j
+                to_x[at] = (part[far_same * group + at].astype(F32)
+                            + from_core[0, at].astype(F32)).astype(BF)
+                return 0
+
+            lax.fori_loop(0, piece, join, 0)
+            over_x(h).start()
+        transform(fi)
+
+    def give_sums():
+        transform(far_other)
+        for h in range(2):
+            to_core(far_other, 0, h).start()
+        transform(core_dev)
+        for h in range(2):
+            to_core(core_dev, 1, h).start()
+
+    for m, (k, g) in enumerate(order):
+        if m + AHEAD < len(order):
+            forward(*order[m + AHEAD])
+        arrive(k, g)
+        correlate(k, g)
+        if k == CHUNKS - 1:
+            if g == 0:
+                table_copy.wait()
+            mine = core == lax.rem(first_block + g, 2)
+            pl.when(mine)(gather_sums)
+            pl.when(jnp.logical_not(mine))(give_sums)
     for h in range(2):
         to_core(core_dev, 1, h).wait_recv()
         over_x(h).wait_recv()
@@ -318,7 +357,8 @@
             pltpu.VMEM(table.shape, BF),
             pltpu.VMEM((bins // CHUNKS * chans, chans), BF),
             pltpu.VMEM((n, bins // 8 * 12 * per, chans), BF),
-            pltpu.VMEM((n, 4 * per, 2 * chans), F32),
+            pltpu.VMEM((n, 2 * per, chans), F32),
+            pltpu.VMEM((2, n, 4 * per, chans), F32),
             pltpu.VMEM((n, 2 * bins * per, chans), BF),
             pltpu.VMEM((n, span, chans), BF),
             pltpu.VMEM((2, group, span, chans), BF),

time: 47.2 us -> 45.3 us (0.960)
  the two profiles are of different devices: /device:TPU:0 before, /device:TPU:1 now
where the time goes in v5:
time: 45.3 us; the launch traced here: 45.1 us
  Pallas kernels  43.4 us (96%)
  local copies, waits for them, and re-layouts  1.04 us (2%)
  between operations  0.66 us (1%)
    pallas_call x1, Pallas kernels, local(): pl.pallas_call(functools.partial(kernel, n), out_shape=jax.ShapeDtypeStru...  42.5 us
    unnamed x4, local copies, waits for them, and re-layouts  1.04 us
    pallas_call x1, Pallas kernels, local(): pl.pallas_call(functools.partial(finish, per), out_shape=(jax.ShapeDtypeS...  0.92 us

profile of v5, /device:TPU:1, one launch (start us, length us, event | category | flops | bytes accessed | tf_op | source)
XLA Modules:
  0.0 45.1 jit_solution(13542286452215218467)
XLA Ops:
  0.6 0.0 copy-start.1
  0.6 42.5 %shard_map.68.total_ref = f32[2,528,128]{2,1,0:T(8,128)} custom-call(s32[4]{0:T(128)} %sources_ref.1, bf16[2,128,96,128]{3,2,1,0:T(8,128)(2,1)} %spectra_ref.1, s32[384,128]{1,0:T(8,128)} %valid_ref.1, bf16[512,1024]{1,0:T(8,128)(2,1)} %constant.2.clone.table_ref), custom_call_target="tpu_custom_call" | custom-call | tf_op jit(solution)/shard_map/pallas_call | solution.py:349
  43.1 0.0 copy-done.1
  43.1 0.0 copy-start
  43.2 1.0 %copy-done = f32[2,528,128]{2,1,0:T(8,128)S(1)} copy-done((f32[2,528,128]{2,1,0:T(8,128)S(1)}, f32[2,528,128]{2,1,0:T(8,128)}, u32[]{:S(2)}) %copy-start) | copy-done | bytes 540696
  44.2 0.9 %shard_map.69 = (bf16[8,128,128]{2,1,0:T(8,128)(2,1)}, f32[8,128]{1,0:T(8,128)}) custom-call(f32[2,528,128]{2,1,0:T(8,128)S(1)} %copy-done, s32[8,2,128]{2,1,0:T(2,128)S(1)} %bitcast.1), custom_call_target="tpu_custom_call" | custom-call | tf_op jit(solution)/shard_map/pallas_call | solution.py:374
Async XLA Ops:
  0.6 42.5 %copy-start.1 = (s32[8,128,2]{1,2,0:T(2,128)S(1)}, s32[8,128,2]{1,2,0:T(2,128)}, u32[]{:S(2)}) copy-start(s32[8,128,2]{1,2,0:T(2,128)} %param.8) | copy-start | bytes 24580
  43.1 1.0 %copy-start = (f32[2,528,128]{2,1,0:T(8,128)S(1)}, f32[2,528,128]{2,1,0:T(8,128)}, u32[]{:S(2)}) copy-start(f32[2,528,128]{2,1,0:T(8,128)} %shard_map.68.total_ref) | copy-start | bytes 1622020

commit v6 on v5

--- a/solution.py
+++ b/solution.py
@@ -12,7 +12,7 @@
 L = 128
 CHUNKS = 8
 EARLY = 3
-AHEAD = 3
+AHEAD = 5
 MESH = pl.DeviceIdType.MESH
 BF = jnp.bfloat16
 F32 = jnp.float32

time: 45.3 us -> 43.3 us (0.956)
  Pallas kernels: 43.4 us -> 41.4 us
    pallas_call x1, Pallas kernels: 42.5 us -> 40.5 us  [local(): pl.pallas_call(functools.partial(kernel, n), out_shape=jax.ShapeDtypeStru...]
where the time goes in v6:
time: 43.3 us; the launch traced here: 43.1 us
  Pallas kernels  41.4 us (96%)
  local copies, waits for them, and re-layouts  1.04 us (2%)
  between operations  0.66 us (2%)
    pallas_call x1, Pallas kernels, local(): pl.pallas_call(functools.partial(kernel, n), out_shape=jax.ShapeDtypeStru...  40.5 us
    unnamed x4, local copies, waits for them, and re-layouts  1.04 us
    pallas_call x1, Pallas kernels, local(): pl.pallas_call(functools.partial(finish, per), out_shape=(jax.ShapeDtypeS...  0.92 us

profile of v6, /device:TPU:1, one launch (start us, length us, event | category | flops | bytes accessed | tf_op | source)
XLA Modules:
  0.0 43.1 jit_solution(16715935271859643446)
XLA Ops:
  0.6 0.0 copy-start.1
  0.6 40.5 %shard_map.68.total_ref = f32[2,528,128]{2,1,0:T(8,128)} custom-call(s32[4]{0:T(128)} %sources_ref.1, bf16[2,128,96,128]{3,2,1,0:T(8,128)(2,1)} %spectra_ref.1, s32[384,128]{1,0:T(8,128)} %valid_ref.1, bf16[512,1024]{1,0:T(8,128)(2,1)} %constant.2.clone.table_ref), custom_call_target="tpu_custom_call" | custom-call | tf_op jit(solution)/shard_map/pallas_call | solution.py:349
  41.1 0.0 copy-done.1
  41.1 0.0 copy-start
  41.2 1.0 %copy-done = f32[2,528,128]{2,1,0:T(8,128)S(1)} copy-done((f32[2,528,128]{2,1,0:T(8,128)S(1)}, f32[2,528,128]{2,1,0:T(8,128)}, u32[]{:S(2)}) %copy-start) | copy-done | bytes 540696
  42.2 0.9 %shard_map.69 = (bf16[8,128,128]{2,1,0:T(8,128)(2,1)}, f32[8,128]{1,0:T(8,128)}) custom-call(f32[2,528,128]{2,1,0:T(8,128)S(1)} %copy-done, s32[8,2,128]{2,1,0:T(2,128)S(1)} %bitcast.1), custom_call_target="tpu_custom_call" | custom-call | tf_op jit(solution)/shard_map/pallas_call | solution.py:374
Async XLA Ops:
  0.6 40.5 %copy-start.1 = (s32[8,128,2]{1,2,0:T(2,128)S(1)}, s32[8,128,2]{1,2,0:T(2,128)}, u32[]{:S(2)}) copy-start(s32[8,128,2]{1,2,0:T(2,128)} %param.8) | copy-start | bytes 24580
  41.1 1.0 %copy-start = (f32[2,528,128]{2,1,0:T(8,128)S(1)}, f32[2,528,128]{2,1,0:T(8,128)}, u32[]{:S(2)}) copy-start(f32[2,528,128]{2,1,0:T(8,128)} %shard_map.68.total_ref) | copy-start | bytes 1622020
